TPU v7x, 32 devices: a whole 2x2x4 slice. The times are simulated.
32 devices in a mesh: dp: 16 (over z, y, x), tensor: 2 (over core).
Axes of the slice: x: 2, y: 2, z: 4, core: 2. Of those that a mesh axis runs over, the one named last changes fastest.
Arguments:
- normed: bfloat16 [8192, 8192], P('dp'), may hold values from -12 to 12
- key_cot: bfloat16 [8192, 256], P('dp', 'tensor'), may hold values from -6 to 6
- key_weight: bfloat16 [8192, 256], P(None, 'tensor'), may hold values from -0.0625 to 0.0625
- norm_gain: bfloat16 [8192], replicated, may hold values from 0.5 to 1.5
- weight_master: float32 [8192, 256], P('dp', 'tensor'), may hold values from -0.0625 to 0.0625
- weight_moment: float32 [8192, 256], P('dp', 'tensor'), may hold values from -0.0041432036 to 0.0041432036
- weight_second: float32 [8192, 256], P('dp', 'tensor'), may hold values from 9.536743e-08 to 2.3841858e-06
- gain_master: float32 [8192], P('dp'), may hold values from 0.5 to 1.5
- gain_moment: float32 [8192], P('dp'), may hold values from -0.0041432036 to 0.0041432036
- gain_second: float32 [8192], P('dp'), may hold values from 9.536743e-08 to 2.3841858e-06
- next_input: bfloat16 [1024, 8192], P('dp'), may hold values from -6 to 6
Outputs:
- next_keys: bfloat16 [1024, 256], P('dp', 'tensor')
- weight_master_new: float32 [8192, 256], P('dp', 'tensor')
- weight_moment_new: float32 [8192, 256], P('dp', 'tensor')
- weight_second_new: float32 [8192, 256], P('dp', 'tensor')
- gain_master_new: float32 [8192], P('dp')
- gain_moment_new: float32 [8192], P('dp')
- gain_second_new: float32 [8192], P('dp')
All inputs are finite; a program needn't handle non-finite values.
Results may differ from a plain program's by a relative error of at most 0.001.
The roundings to bfloat16 on the way count: a program that leaves them out, or rounds other values in their place, can miss the bound.
Values may be sent and summed in bfloat16 or wider, within the bound.
A program may use at most 64 MiB of HBM per device.

v0:
```python
import jax
import jax.numpy as jnp
from jax import lax
from jax.sharding import PartitionSpec as P

beta_one = 0.9
beta_two = 0.95
adam_eps = 1e-08
learn_rate = 0.001
rms_eps = 1e-05
step_count = 10


def adam_update(grad, master, moment, second, decay):
    moment_new = beta_one * moment + (1.0 - beta_one) * grad
    second_new = beta_two * second + (1.0 - beta_two) * grad * grad
    corr_one = 1.0 - beta_one**step_count
    corr_two = 1.0 - beta_two**step_count
    update = moment_new / corr_one / (jnp.sqrt(second_new / corr_two) + adam_eps) + decay * master
    return (master - learn_rate * update, moment_new, second_new)


def bucket_terms(scaled, normed, key_cot, key_weight):
    weight_term = jnp.einsum("td,tc->dc", scaled, key_cot, preferred_element_type=jnp.float32)
    inner = jnp.einsum("td,tc->dc", normed, key_cot, preferred_element_type=jnp.float32)
    gain_term = jnp.sum(key_weight.astype(jnp.float32) * inner, axis=1)
    return (weight_term, gain_term)


def local(
    normed,
    key_cot,
    key_weight,
    norm_gain,
    weight_master,
    weight_moment,
    weight_second,
    gain_master,
    gain_moment,
    gain_second,
    next_input,
):
    heads = lax.axis_size("tensor")
    scaled = (normed.astype(jnp.float32) * norm_gain.astype(jnp.float32)[None, :]).astype(
        jnp.bfloat16
    )
    weight_term, gain_term = bucket_terms(scaled, normed, key_cot, key_weight)
    key_grad, gain_part = (
        lax.psum_scatter(weight_term, "dp", scatter_dimension=0, tiled=True),
        lax.psum_scatter(gain_term, "dp", scatter_dimension=0, tiled=True),
    )
    gain_grad = lax.psum(gain_part, "tensor")
    local_sum = jnp.sum(key_grad * key_grad) + jnp.sum(gain_grad * gain_grad) / heads
    total = lax.psum(local_sum, ("dp", "tensor"))
    clip = jnp.minimum(1.0, 1.0 / (jnp.sqrt(total) + 1e-06))
    weight_new, weight_moment_new, weight_second_new = adam_update(
        clip * key_grad, weight_master, weight_moment, weight_second, 0.1
    )
    gain_new, gain_moment_new, gain_second_new = adam_update(
        clip * gain_grad, gain_master, gain_moment, gain_second, 0.0
    )
    weight_param = weight_new.astype(jnp.bfloat16)
    gain_param = gain_new.astype(jnp.bfloat16)
    hidden = next_input.astype(jnp.float32)
    inverse = lax.rsqrt(jnp.mean(hidden * hidden, axis=1, keepdims=True) + rms_eps)
    rescaled = hidden * inverse
    weight_piece = lax.all_gather(weight_param, "dp", axis=0, tiled=True)
    gain_piece = lax.all_gather(gain_param, "dp", axis=0, tiled=True)
    mixed = (rescaled * gain_piece.astype(jnp.float32)[None, :]).astype(jnp.bfloat16)
    next_keys = jnp.dot(mixed, weight_piece, preferred_element_type=jnp.float32)
    return (
        next_keys.astype(jnp.bfloat16),
        weight_new,
        weight_moment_new,
        weight_second_new,
        gain_new,
        gain_moment_new,
        gain_second_new,
    )


def solution(mesh):
    return jax.shard_map(
        local,
        mesh=mesh,
        in_specs=(
            P("dp", None),
            P("dp", "tensor"),
            P(None, "tensor"),
            P(),
            P("dp", "tensor"),
            P("dp", "tensor"),
            P("dp", "tensor"),
            P("dp"),
            P("dp"),
            P("dp"),
            P("dp", None),
        ),
        out_specs=(
            P("dp", "tensor"),
            P("dp", "tensor"),
            P("dp", "tensor"),
            P("dp", "tensor"),
            P("dp"),
            P("dp"),
            P("dp"),
        ),
        check_vma=False,
    )
```

profile of v0, /device:TPU:0, one launch (start us, length us, event | category | flops | bytes accessed | tf_op | source)
XLA Modules:
  0.0 231.8 jit_solution(1057078759068094781)
XLA Ops:
  7.2 0.0 copy-start
  7.2 0.0 reduce-scatter.2.cloned.1.call-start
  7.2 0.8 convert_element_type.32
  8.0 0.1 copy-done
  8.1 7.8 %fusion = f32[8192,128]{1,0:T(8,128)} fusion(bf16[512,128]{1,0:T(8,128)(2,1)S(1)} %copy-done, bf16[512,8192]{1,0:T(8,128)(2,1)} %param.11, f32[8192]{0:T(1024)S(1)} %convert_element_type.32), kind=kOutput, calls=%fused_computation.2 | convolution fusion | flops 1086324736 | bytes 12746752 | tf_op jit(solution)/shard_map/td,tc->dc/dot_general | solution.py:24
  15.9 0.0 copy-start.1
  15.9 0.0 copy-start.9
  15.9 0.0 reduce-scatter.2.cloned.1.call-update
  15.9 0.0 all-gather.3.cloned.1.call-start
  16.0 1.5 copy-done.1
  17.5 3.0 %copy.19 = bf16[8192,128]{0,1:T(8,128)(2,1)} copy(bf16[8192,128]{1,0:T(8,128)(2,1)S(1)} %copy-done.1) | data formatting | bytes 4194304 | tf_op args[2]
  20.5 0.0 copy-done.9
  20.5 0.6 dynamic-slice
  21.7 0.0 copy-start.3
  21.7 0.0 copy-start.4
  21.7 0.0 copy-start.5
  21.8 0.0 copy-start.2
  21.8 0.0 copy-start.6
  21.8 0.0 copy-start.7
  21.8 0.0 copy-start.8
  21.8 6.0 %fusion.5 = f32[8192]{0:T(1024)S(1)} fusion(bf16[512,8192]{1,0:T(8,128)(2,1)} %param.11, bf16[512,128]{1,0:T(8,128)(2,1)S(1)} %copy-done, bf16[8192,128]{0,1:T(8,128)(2,1)} %copy.19), kind=kOutput, calls=%fused_computation.9 | convolution fusion | flops 1076879360 | bytes 10649600 | tf_op jit(solution)/shard_map/td,tc->dc/dot_general | solution.py:25
  27.8 78.8 %all-reduce = f32[8192]{0:T(1024)S(1)} all-reduce(f32[8192]{0:T(1024)S(1)} %fusion.5), channel_id=3, replica_groups=mesh['dp'=16,'tensor'=2] {'dp'}, use_global_device_ids=true, to_apply=%region_4.0.clone | all-reduce | flops 8192 | bytes 65536
  106.6 0.1 dynamic-slice.1
  106.7 2.4 %psum.14 = f32[512]{0:T(512)S(1)} all-reduce(f32[512]{0:T(512)S(1)} %dynamic-slice.1), channel_id=1, replica_groups=mesh['dp'=16,'tensor'=2] {'tensor'}, use_global_device_ids=true, to_apply=%region_5.0 | all-reduce | flops 512 | bytes 4096 | tf_op jit(solution)/shard_map/psum | solution.py:52
  109.1 0.6 multiply_reduce_fusion.1
  110.4 6.1 %reduce-scatter.2.cloned.1.call-done = f32[512,128]{1,0:T(8,128)} async-done(((f32[8192,128]{1,0:T(8,128)}), f32[512,128]{1,0:T(8,128)}) %reduce-scatter.2.cloned.1.call-update) | async-done | bytes 262160 | tf_op jit(solution)/shard_map/reduce_scatter | solution.py:49
  116.5 1.6 multiply_reduce_fusion
  118.7 39.1 %psum.15 = f32[]{:T(128)} all-reduce(f32[]{:T(128)S(6)} %add.57), channel_id=1, replica_groups=mesh['dp'=16,'tensor'=2] {'dp','tensor'}, use_global_device_ids=true, to_apply=%region_7.0 | all-reduce | flops 1 | bytes 8 | tf_op jit(solution)/shard_map/psum | solution.py:54
  158.6 0.0 copy-done.3
  158.6 0.0 copy-done.4
  158.6 0.0 copy-done.5
  158.6 2.0 fusion.13
  160.6 0.0 all-gather.3.cloned.1.call-update
  160.6 0.0 copy-done.2
  160.6 0.3 fusion.2
  161.0 0.0 copy-done.6
  161.0 0.0 copy-done.7
  161.0 0.0 copy-done.8
  161.0 0.6 fusion.11
  161.6 40.5 %all-gather = bf16[16,1,512]{2,1,0:T(2,128)(2,1)S(1)} all-gather(bf16[1,1,512]{2,1,0:T(2,128)(2,1)S(1)} %reshape.24), channel_id=1, replica_groups=mesh['dp'=16,'tensor'=2] {'dp'}, dimensions={0}, use_global_device_ids=true | all-gather | bytes 17408 | tf_op jit(solution)/shard_map/all_gather | solution.py:68
  202.1 20.1 %all-gather.3.cloned.1.call-done = bf16[8192,128]{1,0:T(8,128)(2,1)} async-done(((bf16[512,128]{1,0:T(8,128)(2,1)}), bf16[8192,128]{1,0:T(8,128)(2,1)}) %all-gather.3.cloned.1.call-update) | async-done | bytes 2097168 | tf_op jit(solution)/shard_map/all_gather | solution.py:67
  222.3 2.7 %convolution_convert_fusion = bf16[64,128]{1,0:T(8,128)(2,1)} fusion(bf16[8192,128]{1,0:T(8,128)(2,1)} %all-gather.3.cloned.1.call-done, bf16[64,8192]{1,0:T(8,128)(2,1)S(1)} %copy-done.2, f32[8192]{0:T(1024)S(1)} %bitcast.6, f32[64]{0:T(128)S(1)} %add_rsqrt_fusion), kind=kOutput, calls=%fused_computation.10 | convolution fusion | flops 136323072 | bytes 3195136 | tf_op jit(solution)/shard_map/dot_general | solution.py:70
  (3 shorter events, 0.0 us)
Async XLA Ops:
  7.2 0.9 copy-start
  7.2 109.3 %reduce-scatter.2.cloned.1.call-start = ((), (), s32[]{:S(2)}) async-start(), calls=%async_computation.1 | async-start | bytes 4456448 | tf_op jit(solution)/shard_map/reduce_scatter | solution.py:49
  15.9 1.6 copy-start.1
  15.9 4.6 %copy-start.9 = (u32[32]{0:T(128)S(1)}, u32[32]{0:T(128)}, u32[]{:S(2)}) copy-start(u32[32]{0:T(128)} %constant.13) | copy-start | bytes 388
  15.9 206.3 %all-gather.3.cloned.1.call-start = ((), (), s32[]{:S(2)}) async-start(), calls=%async_computation.2 | async-start | bytes 2228224 | tf_op jit(solution)/shard_map/all_gather | solution.py:67
  21.7 136.9 %copy-start.3 = (f32[512,128]{1,0:T(8,128)S(1)}, f32[512,128]{1,0:T(8,128)}, u32[]{:S(2)}) copy-start(f32[512,128]{1,0:T(8,128)} %param.15) | copy-start | bytes 786436
  21.7 136.9 %copy-start.4 = (f32[512,128]{1,0:T(8,128)S(1)}, f32[512,128]{1,0:T(8,128)}, u32[]{:S(2)}) copy-start(f32[512,128]{1,0:T(8,128)} %param.16) | copy-start | bytes 786436
  21.7 136.9 %copy-start.5 = (f32[512,128]{1,0:T(8,128)S(1)}, f32[512,128]{1,0:T(8,128)}, u32[]{:S(2)}) copy-start(f32[512,128]{1,0:T(8,128)} %param.17) | copy-start | bytes 786436
  21.8 138.9 %copy-start.2 = (bf16[64,8192]{1,0:T(8,128)(2,1)S(1)}, bf16[64,8192]{1,0:T(8,128)(2,1)}, u32[]{:S(2)}) copy-start(bf16[64,8192]{1,0:T(8,128)(2,1)} %param.21) | copy-start | bytes 3145732
  21.8 139.2 %copy-start.6 = (f32[512]{0:T(512)S(1)}, f32[512]{0:T(512)}, u32[]{:S(2)}) copy-start(f32[512]{0:T(512)} %param.18) | copy-start | bytes 6148
  21.8 139.2 %copy-start.7 = (f32[512]{0:T(512)S(1)}, f32[512]{0:T(512)}, u32[]{:S(2)}) copy-start(f32[512]{0:T(512)} %param.19) | copy-start | bytes 6148
  21.8 139.2 %copy-start.8 = (f32[512]{0:T(512)S(1)}, f32[512]{0:T(512)}, u32[]{:S(2)}) copy-start(f32[512]{0:T(512)} %param.20) | copy-start | bytes 6148
Sparse Core Ops, SparseCore 0:
  16.1 100.3 reduce-scatter.1
  160.8 61.4 all-gather.2
where the time goes:
time: 232 us
  blocking collectives  161 us (69%)
  waiting for transfers between devices  26.2 us (11%)
  between operations  16.9 us (7%)
  matrix products  16.5 us (7%)
  other arithmetic  5.93 us (3%)
  local copies, waits for them, and re-layouts  5.29 us (2%)
    unnamed x1, blocking collectives  78.8 us
    all_gather x1, blocking collectives, local(): gain_piece = lax.all_gather(gain_param, 'dp', axis=0, tiled=True)  40.5 us
    psum x1, blocking collectives, local(): total = lax.psum(local_sum, ('dp', 'tensor'))  39.1 us
    all_gather x1, waiting for transfers between devices, local(): weight_piece = lax.all_gather(weight_param, 'dp', axis=0, tiled=True)  20.1 us
    dot_general x1, matrix products, bucket_terms(): jnp.einsum('td,tc->dc', scaled, key_cot, preferred_element_type=jnp.float32)  7.83 us
    reduce_scatter x1, waiting for transfers between devices, local(): lax.psum_scatter(weight_term, 'dp', scatter_dimension=0, tiled=True)  6.08 us
    dot_general x1, matrix products, bucket_terms(): jnp.einsum('td,tc->dc', normed, key_cot, preferred_element_type=jnp.float32)  6 us
    unnamed x24, local copies, waits for them, and re-layouts  5.29 us
  transfers between devices with their start and end apart: 2, of which 2 were waited for; matrix products, arithmetic and copies ran while one was open for 5% of the time, Pallas kernels for 0%

commit v1 on v0

v1 whole, which is shorter than its diff:
```python
import functools

import jax
import jax.numpy as jnp
from jax import lax
from jax.experimental import pallas as pl
from jax.experimental.pallas import tpu as pltpu
from jax.sharding import PartitionSpec as P

beta_one = 0.9
beta_two = 0.95
adam_eps = 1e-08
learn_rate = 0.001
rms_eps = 1e-05
step_count = 10
MESH = pl.DeviceIdType.MESH


def adam_update(grad, master, moment, second, decay):
    moment_new = beta_one * moment + (1.0 - beta_one) * grad
    second_new = beta_two * second + (1.0 - beta_two) * grad * grad
    corr_one = 1.0 - beta_one**step_count
    corr_two = 1.0 - beta_two**step_count
    update = moment_new / corr_one / (jnp.sqrt(second_new / corr_two) + adam_eps) + decay * master
    return (master - learn_rate * update, moment_new, second_new)


def encode(value):
    return (value * jnp.abs(value) * (value * value)).astype(jnp.bfloat16)


def decode(coded):
    power = coded.astype(jnp.float32)
    size = jnp.maximum(jnp.abs(power), 1.2e-38)
    root = lax.rsqrt(size)
    return power * root * lax.rsqrt(size * root)


def kernel(
    dims,
    normed, cot_in, weight_in, gains, gain_in, master_in, moment_in, second_in,
    gmaster, gmoment, gsecond, next_in, next_blocks,
    keys_out, master_out, moment_out, second_out, gmaster_out, gmoment_out, gsecond_out,
    xbuf, cot, kw, master, moment, second, rows_in, prod, got1, give2, got2,
    hbuf, resc, inv_all, gain_all, total_all, part, got_part,
    x_sem, in_sem, own_sem, s1, r1, s2, r2, sh, rh, sm, rm, si, ri, sg, rg, st, rt, sp, rp,
):
    n, heads, q, m, size, width, group, chunks, rows, half_rows = dims
    me = lax.axis_index("dp")
    ten = lax.axis_index("tensor")
    mp = lax.rem(me, q)
    mz = lax.div(me, q)
    half = lax.rem(ten, 2)
    mate = ten + 1 - 2 * half

    def x_copy(c):
        at = pl.ds(pl.multiple_of(c * width, 128), width)
        return pltpu.make_async_copy(normed.at[:, at], xbuf.at[c], x_sem.at[c])

    def loop(low, high, body):
        def step(i, carry):
            body(i)
            return carry

        lax.fori_loop(low, high, step, 0)

    def peer(k):
        return lax.rem(mp + k, q)

    def plane(j):
        return lax.rem(mz + j, m)

    cot_copy = pltpu.make_async_copy(cot_in, cot, in_sem.at[0])
    cot_copy.start()
    if group == 1:

        def fetch(j):
            for k in range(1, q):
                x_copy(plane(j) * q + peer(k)).start()

        loop(1, m + 1, fetch)
        loop(1, m + 1, lambda j: x_copy(plane(j) * q + mp).start())
    else:
        loop(0, chunks, lambda c: x_copy(c).start())
    own_rows = pl.ds(pl.multiple_of(me * size, 16), size)
    local_copies = [
        pltpu.make_async_copy(next_in, rows_in, in_sem.at[1]),
        pltpu.make_async_copy(weight_in.at[own_rows], kw, in_sem.at[2]),
        pltpu.make_async_copy(master_in, master, in_sem.at[3]),
        pltpu.make_async_copy(moment_in, moment, in_sem.at[4]),
        pltpu.make_async_copy(second_in, second, in_sem.at[5]),
    ]
    for copy in local_copies:
        copy.start()

    my_half = pl.ds(pl.multiple_of(half * half_rows, 16), half_rows)

    def next_block(dest):
        if group == 1:
            at = pl.ds(pl.multiple_of(dest * size, 128), size)
            return next_blocks.at[my_half, at]
        return next_blocks.at[dest, my_half]

    own_block = pltpu.make_async_copy(next_block(me), hbuf.at[half, me], own_sem)
    own_block.start()

    barrier = pltpu.get_barrier_semaphore()

    def other(j):
        return lax.rem(me + j, n)

    def greet(j):
        pl.semaphore_signal(barrier, inc=1, device_id=(other(j), ten), device_id_type=MESH)

    loop(1, n, greet)
    for t in range(1, heads):
        pl.semaphore_signal(
            barrier, inc=1, device_id=(me, lax.rem(ten + t, heads)), device_id_type=MESH
        )
    pl.semaphore_wait(barrier, n - 1 + heads - 1)

    def remote(src, dst, send, recv, dev):
        return pltpu.make_async_remote_copy(
            src_ref=src, dst_ref=dst, send_sem=send, recv_sem=recv,
            device_id=dev, device_id_type=MESH,
        )

    def h_copy(j):
        return remote(
            next_block(other(j)), hbuf.at[half, me], sh.at[j], rh.at[j], (other(j), ten)
        )

    loop(1, n, lambda j: h_copy(j).start())

    cot_copy.wait()
    cot_t = cot[...].astype(jnp.float32).T.astype(jnp.bfloat16)

    def product(c):
        x_copy(c).wait()
        scaled = (xbuf[c].astype(jnp.float32) * gains[c]).astype(jnp.bfloat16)
        y = jnp.dot(cot_t, scaled, preferred_element_type=jnp.float32).T
        for g in range(group):
            prod[c * group + g] = encode(y[g * size : (g + 1) * size])

    def copy1(j, k):
        z = plane(j)
        return remote(
            prod.at[z * q + peer(k)], got1.at[(k - 1) * m + z],
            s1.at[(k - 1) * m + z], r1.at[(k - 1) * m + z], (mz * q + peer(k), ten),
        )

    if group > 1:
        loop(0, chunks, product)

    def stage1(j):
        for k in range(1, q):
            if group == 1:
                product(plane(j) * q + peer(k))
            copy1(j, k).start()

    loop(1, m + 1, stage1)

    local_copies[0].wait()
    total_row = jnp.zeros((rows, 128), jnp.float32)
    depth = rows_in.shape[1]
    for at in range(0, depth, 1024):
        piece = rows_in[:, at : at + 1024].astype(jnp.float32)
        piece = piece * piece
        for lane in range(0, 1024, 128):
            total_row = total_row + piece[:, lane : lane + 128]
    inverse = lax.rsqrt(jnp.sum(total_row, axis=1, keepdims=True) / depth + rms_eps)
    square = jnp.broadcast_to(inverse, (rows, 128))
    if rows < 128:
        square = jnp.concatenate([square, jnp.zeros((128 - rows, 128), jnp.float32)], axis=0)
    inv_all[me] = square.T[0:8]

    def i_copy(j):
        return remote(inv_all.at[me], inv_all.at[me], si.at[j], ri.at[j], (other(j), ten))

    loop(1, n, lambda j: i_copy(j).start())

    if group == 1:
        loop(1, m + 1, lambda j: product(plane(j) * q + mp))

    def copy2(j):
        return remote(
            give2.at[j], got2.at[j], s2.at[j], r2.at[j], (plane(j) * q + mp, ten)
        )

    def plane_sum(j):
        total = decode(prod[plane(j) * q + mp])
        for k in range(1, q):
            copy1(j, k).wait_recv()
            total = total + decode(got1[(k - 1) * m + plane(j)])
        return total

    def stage2(j):
        give2[j] = encode(plane_sum(j))
        copy2(j).start()

    loop(1, m, stage2)

    own_block.wait()
    loop(1, n, lambda j: h_copy(j).wait_recv())
    mate_give = remote(hbuf.at[half], hbuf.at[half], sm, rm, (me, mate))
    mate_take = remote(hbuf.at[1 - half], hbuf.at[1 - half], sm, rm, (me, mate))
    mate_give.start()

    key_grad = plane_sum(m)
    for copy in local_copies[1:]:
        copy.wait()
    kw_t = kw[...].astype(jnp.float32).T / gain_in[me]

    loop(1, n, lambda j: i_copy(j).wait_recv())
    mate_take.wait_recv()

    def rescale(s):
        column = jnp.broadcast_to(inv_all[s][0:1], (128, 128)).T[:rows, 0:1]
        for h in range(2):
            at = slice(h * half_rows, (h + 1) * half_rows)
            resc[s, at] = hbuf[h, s].astype(jnp.float32) * column[at]

    loop(0, n, rescale)

    for j in range(1, m):
        copy2(j).wait_recv()
        key_grad = key_grad + decode(got2[j])

    grad_t = key_grad.T
    gain_all[ten, 0:1] = jnp.sum(kw_t * grad_t, axis=0, keepdims=True)
    gain_all[ten, 1:2] = jnp.sum(grad_t * grad_t, axis=0, keepdims=True)

    def g_copy(t):
        dev = (me, lax.rem(ten + t, heads))
        return remote(gain_all.at[ten], gain_all.at[ten], sg.at[t], rg.at[t], dev)

    for t in range(1, heads):
        g_copy(t).start()
    for t in range(1, heads):
        g_copy(t).wait_recv()
    gain_grad = gain_all[0, 0:1]
    squares = gain_all[0, 1:2]
    for t in range(1, heads):
        gain_grad = gain_grad + gain_all[t, 0:1]
        squares = squares + gain_all[t, 1:2]
    squares = squares + gain_grad * gain_grad
    total_all[me] = jnp.broadcast_to(jnp.sum(squares, axis=1, keepdims=True), (8, 128))

    def t_copy(j):
        return remote(total_all.at[me], total_all.at[me], st.at[j], rt.at[j], (other(j), ten))

    loop(1, n, lambda j: t_copy(j).start())
    loop(1, n, lambda j: t_copy(j).wait_recv())
    total = jnp.sum(total_all[...], axis=0)
    clip = jnp.minimum(1.0, 1.0 / (jnp.sqrt(total) + 1e-06))[0:1]

    master_new, moment_new, second_new = adam_update(
        key_grad * clip, master[...], moment[...], second[...], 0.1
    )
    master_out[...] = master_new
    moment_out[...] = moment_new
    second_out[...] = second_new
    weight = master_new.astype(jnp.bfloat16)
    gain_new, gain_moment_new, gain_second_new = adam_update(
        gain_grad * clip[:, 0:1], gmaster[...], gmoment[...], gsecond[...], 0.0
    )
    gmaster_out[...] = gain_new
    gmoment_out[...] = gain_moment_new
    gsecond_out[...] = gain_second_new
    gain = gain_new.astype(jnp.bfloat16).astype(jnp.float32)

    def keys(s):
        mixed = (resc[s] * gain).astype(jnp.bfloat16)
        return jnp.dot(mixed, weight, preferred_element_type=jnp.float32)

    def p_copy(j):
        return remote(part.at[j], got_part.at[j], sp.at[j], rp.at[j], (other(j), ten))

    def share(j):
        part[j] = keys(other(j))
        p_copy(j).start()

    loop(1, n, share)
    part[0] = keys(me)

    def collect(j):
        p_copy(j).wait_recv()
        part[0] = part[0] + got_part[j]

    loop(1, n, collect)
    keys_out[...] = part[0].astype(jnp.bfloat16)

    def drain(j):
        h_copy(j).wait_send()
        i_copy(j).wait_send()
        t_copy(j).wait_send()
        p_copy(j).wait_send()

    loop(1, n, drain)

    def drain1(j):
        for k in range(1, q):
            copy1(j, k).wait_send()

    loop(1, m + 1, drain1)
    loop(1, m, lambda j: copy2(j).wait_send())
    mate_give.wait_send()
    for t in range(1, heads):
        g_copy(t).wait_send()


def local(
    normed,
    key_cot,
    key_weight,
    norm_gain,
    weight_master,
    weight_moment,
    weight_second,
    gain_master,
    gain_moment,
    gain_second,
    next_input,
):
    n = lax.axis_size("dp")
    heads = lax.axis_size("tensor")
    tokens, depth = normed.shape
    size = depth // n
    cols = key_cot.shape[1]
    rows = next_input.shape[0]
    half_rows = rows // 2
    q = 4 if n % 4 == 0 else 1
    m = n // q
    width = size if size % 128 == 0 else 512
    group = width // size
    chunks = depth // width
    dims = (n, heads, q, m, size, width, group, chunks, rows, half_rows)
    if group == 1:
        blocks = next_input
    else:
        blocks = next_input.reshape(rows, n, size).transpose(1, 0, 2)
    gain = norm_gain.astype(jnp.float32)
    hbm = pl.BlockSpec(memory_space=pl.ANY)
    vmem = pl.BlockSpec(memory_space=pltpu.VMEM)
    f32, bf16 = jnp.float32, jnp.bfloat16
    dma = pltpu.SemaphoreType.DMA
    shard = jax.ShapeDtypeStruct((size, cols), f32)
    line = jax.ShapeDtypeStruct((1, size), f32)
    outs = pl.pallas_call(
        functools.partial(kernel, dims),
        out_shape=(
            jax.ShapeDtypeStruct((rows, cols), bf16), shard, shard, shard, line, line, line,
        ),
        in_specs=[hbm, hbm, hbm, vmem, vmem, hbm, hbm, hbm, vmem, vmem, vmem, hbm, hbm],
        out_specs=(vmem,) * 7,
        scratch_shapes=[
            pltpu.VMEM((chunks, tokens, width), bf16),
            pltpu.VMEM((tokens, cols), bf16),
            pltpu.VMEM((size, cols), bf16),
            pltpu.VMEM((size, cols), f32),
            pltpu.VMEM((size, cols), f32),
            pltpu.VMEM((size, cols), f32),
            pltpu.VMEM((rows, depth), bf16),
            pltpu.VMEM((n, size, cols), bf16),
            pltpu.VMEM((max(q - 1, 1) * m, size, cols), bf16),
            pltpu.VMEM((m, size, cols), bf16),
            pltpu.VMEM((m, size, cols), bf16),
            pltpu.VMEM((2, n, half_rows, size), bf16),
            pltpu.VMEM((n, rows, size), f32),
            pltpu.VMEM((n, 8, 128), f32),
            pltpu.VMEM((heads, 8, size), f32),
            pltpu.VMEM((n, 8, 128), f32),
            pltpu.VMEM((n, rows, cols), f32),
            pltpu.VMEM((n, rows, cols), f32),
            dma((chunks,)), dma((6,)), dma,
            dma((max(q - 1, 1) * m,)), dma((max(q - 1, 1) * m,)),
            dma((m,)), dma((m,)),
            dma((n,)), dma((n,)),
            dma, dma,
            dma((n,)), dma((n,)),
            dma((heads,)), dma((heads,)),
            dma((n,)), dma((n,)),
            dma((n,)), dma((n,)),
        ],
        compiler_params=pltpu.CompilerParams(
            collective_id=0, has_side_effects=True, vmem_limit_bytes=52 * 1024 * 1024
        ),
        cost_estimate=pl.CostEstimate(
            flops=2 * tokens * depth * cols + 2 * n * rows * size * cols,
            bytes_accessed=2 * tokens * depth,
            transcendentals=0,
        ),
    )(
        normed, key_cot, key_weight,
        gain.reshape(chunks, 1, width), gain.reshape(n, 1, size), weight_master, weight_moment, weight_second,
        gain_master.reshape(1, size), gain_moment.reshape(1, size),
        gain_second.reshape(1, size), next_input, blocks,
    )
    keys, master, moment, second, gmaster, gmoment, gsecond = outs
    return (
        keys, master, moment, second,
        gmaster.reshape(size), gmoment.reshape(size), gsecond.reshape(size),
    )


def solution(mesh):
    return jax.shard_map(
        local,
        mesh=mesh,
        in_specs=(
            P("dp", None),
            P("dp", "tensor"),
            P(None, "tensor"),
            P(),
            P("dp", "tensor"),
            P("dp", "tensor"),
            P("dp", "tensor"),
            P("dp"),
            P("dp"),
            P("dp"),
            P("dp", None),
        ),
        out_specs=(
            P("dp", "tensor"),
            P("dp", "tensor"),
            P("dp", "tensor"),
            P("dp", "tensor"),
            P("dp"),
            P("dp"),
            P("dp"),
        ),
        check_vma=False,
    )
```

time: 232 us -> 72.5 us (0.31)
  the two profiles are of different devices: /device:TPU:0 before, /device:TPU:14 now
where the time goes in v1:
time: 72.5 us; the launch traced here: 72.1 us
  Pallas kernels  60.5 us (83%)
  local copies, waits for them, and re-layouts  10.2 us (14%)
    pallas_call x1, Pallas kernels, local(): pl.pallas_call(functools.partial(kernel, dims), out_shape=(jax.ShapeDtype...  60.5 us
    unnamed x21, local copies, waits for them, and re-layouts  10.2 us

profile of v1, /device:TPU:14, one launch (start us, length us, event | category | flops | bytes accessed | tf_op | source)
XLA Modules:
  0.0 72.1 jit_solution(17271687229999494448)
XLA Ops:
  0.6 0.7 %reshape.46 = f32[8192]{0:T(1024)S(1)} convert(bf16[8192]{0:T(1024)(128)(2,1)} %param.14) | non-fusion elementwise | flops 8192 | bytes 49152 | tf_op jit(solution)/shard_map/reshape | solution.py:395
  1.4 0.0 copy-start
  1.4 0.9 %copy-done = f32[512,128]{1,0:T(8,128)S(1)} copy-done((f32[512,128]{1,0:T(8,128)S(1)}, f32[512,128]{1,0:T(8,128)}, u32[]{:S(2)}) %copy-start) | copy-done | bytes 262168
  2.3 0.0 copy-start.1
  2.3 0.9 %copy-done.1 = f32[512,128]{1,0:T(8,128)S(1)} copy-done((f32[512,128]{1,0:T(8,128)S(1)}, f32[512,128]{1,0:T(8,128)}, u32[]{:S(2)}) %copy-start.1) | copy-done | bytes 262168
  3.3 0.0 copy-start.2
  3.3 0.9 %copy-done.2 = f32[512,128]{1,0:T(8,128)S(1)} copy-done((f32[512,128]{1,0:T(8,128)S(1)}, f32[512,128]{1,0:T(8,128)}, u32[]{:S(2)}) %copy-start.2) | copy-done | bytes 262168
  4.2 0.0 copy-start.3
  4.2 0.9 %copy-done.3 = bf16[512,128]{1,0:T(8,128)(2,1)S(1)} copy-done((bf16[512,128]{1,0:T(8,128)(2,1)S(1)}, bf16[512,128]{1,0:T(8,128)(2,1)}, u32[]{:S(2)}) %copy-start.3) | copy-done | bytes 131096
  5.1 0.0 copy-start.4
  5.1 0.7 copy-done.4
  5.8 0.0 copy-start.5
  5.8 0.7 copy-done.5
  6.5 0.0 copy-start.6
  6.5 0.7 copy-done.6
  7.2 60.5 %shard_map.162 = (bf16[64,128]{1,0:T(8,128)(2,1)S(1)}, f32[512,128]{1,0:T(8,128)S(1)}, f32[512,128]{1,0:T(8,128)S(1)}, f32[512,128]{1,0:T(8,128)S(1)}, f32[1,512...) custom-call(bf16[512,8192]{1,0:T(8,128)(2,1)} %normed.1, bf16[512,128]{1,0:T(8,128)(2,1)S(1)} %copy-done.3, ...), custom_call_target="tpu_custom_call" | custom-call | flops 1207959552 | bytes 8388608 | tf_op jit(solution)/shard_map/pallas_call | solution.py:349
  67.7 0.6 copy.25
  68.3 0.7 copy.26
  69.0 0.7 copy.27
  69.7 0.7 copy.28
  70.4 0.6 copy.29
  71.0 0.6 copy.30
  71.5 0.6 copy.31
Async XLA Ops:
  1.4 0.9 %copy-start = (f32[512,128]{1,0:T(8,128)S(1)}, f32[512,128]{1,0:T(8,128)}, u32[]{:S(2)}) copy-start(f32[512,128]{1,0:T(8,128)} %master_in.1) | copy-start | bytes 786436
  2.3 0.9 %copy-start.1 = (f32[512,128]{1,0:T(8,128)S(1)}, f32[512,128]{1,0:T(8,128)}, u32[]{:S(2)}) copy-start(f32[512,128]{1,0:T(8,128)} %moment_in.1) | copy-start | bytes 786436
  3.3 0.9 %copy-start.2 = (f32[512,128]{1,0:T(8,128)S(1)}, f32[512,128]{1,0:T(8,128)}, u32[]{:S(2)}) copy-start(f32[512,128]{1,0:T(8,128)} %second_in.1) | copy-start | bytes 786436
  4.2 0.9 %copy-start.3 = (bf16[512,128]{1,0:T(8,128)(2,1)S(1)}, bf16[512,128]{1,0:T(8,128)(2,1)}, u32[]{:S(2)}) copy-start(bf16[512,128]{1,0:T(8,128)(2,1)} %cot_in.1) | copy-start | bytes 393220
  5.1 0.7 copy-start.4
  5.8 0.7 copy-start.5
  6.5 0.7 copy-start.6

commit v2 on v1

--- a/solution.py
+++ b/solution.py
@@ -38,12 +38,14 @@
 
 def kernel(
     dims,
-    normed, cot_in, weight_in, gains, gain_in, master_in, moment_in, second_in,
-    gmaster, gmoment, gsecond, next_in, next_blocks,
+    normed, cot_in, weight_in, gains_in, gain_in_hbm, master_in, moment_in, second_in,
+    gmaster_in, gmoment_in, gsecond_in, next_in, next_blocks,
     keys_out, master_out, moment_out, second_out, gmaster_out, gmoment_out, gsecond_out,
     xbuf, cot, kw, master, moment, second, rows_in, prod, got1, give2, got2,
-    hbuf, resc, inv_all, gain_all, total_all, part, got_part,
-    x_sem, in_sem, own_sem, s1, r1, s2, r2, sh, rh, sm, rm, si, ri, sg, rg, st, rt, sp, rp,
+    hbuf, resc, inv_all, gain_all, total_all, part, got_part, give_keys, got_keys,
+    gains, gain_in, gmaster, gmoment, gsecond, keys_v, master_v, moment_v, second_v,
+    gmaster_v, gmoment_v, gsecond_v,
+    x_sem, in_sem, own_sem, s1, r1, s2, r2, sh, rh, sm, rm, si, ri, sg, rg, st, rt, sp, rp, s3, r3, out_sem,
 ):
     n, heads, q, m, size, width, group, chunks, rows, half_rows = dims
     me = lax.axis_index("dp")
@@ -70,15 +72,31 @@
     def plane(j):
         return lax.rem(mz + j, m)
 
+    across = lax.rem(mp, 2)
+    along = lax.div(mp, 2)
+    in_row = 1 - across + 2 * along
+    in_column = across + 2 * (1 - along)
+    diagonal = 3 - mp
+
+    def near_one(j):
+        return in_column + (in_row - in_column) * lax.rem(j, 2)
+
+    def near_two(j):
+        return in_row + (in_column - in_row) * lax.rem(j, 2)
+
     cot_copy = pltpu.make_async_copy(cot_in, cot, in_sem.at[0])
     cot_copy.start()
+    gains_copy = pltpu.make_async_copy(gains_in, gains, in_sem.at[6])
+    gains_copy.start()
     if group == 1:
 
         def fetch(j):
-            for k in range(1, q):
-                x_copy(plane(j) * q + peer(k)).start()
-
-        loop(1, m + 1, fetch)
+            x_copy(plane(j) * q + diagonal).start()
+            x_copy(plane(j) * q + near_one(j)).start()
+
+        if q > 1:
+            loop(1, m + 1, fetch)
+            loop(1, m + 1, lambda j: x_copy(plane(j) * q + near_two(j)).start())
         loop(1, m + 1, lambda j: x_copy(plane(j) * q + mp).start())
     else:
         loop(0, chunks, lambda c: x_copy(c).start())
@@ -89,6 +107,10 @@
         pltpu.make_async_copy(master_in, master, in_sem.at[3]),
         pltpu.make_async_copy(moment_in, moment, in_sem.at[4]),
         pltpu.make_async_copy(second_in, second, in_sem.at[5]),
+        pltpu.make_async_copy(gain_in_hbm.at[me], gain_in, in_sem.at[7]),
+        pltpu.make_async_copy(gmaster_in, gmaster, in_sem.at[8]),
+        pltpu.make_async_copy(gmoment_in, gmoment, in_sem.at[9]),
+        pltpu.make_async_copy(gsecond_in, gsecond, in_sem.at[10]),
     ]
     for copy in local_copies:
         copy.start()
@@ -133,32 +155,51 @@
     loop(1, n, lambda j: h_copy(j).start())
 
     cot_copy.wait()
+    gains_copy.wait()
     cot_t = cot[...].astype(jnp.float32).T.astype(jnp.bfloat16)
 
     def product(c):
         x_copy(c).wait()
         scaled = (xbuf[c].astype(jnp.float32) * gains[c]).astype(jnp.bfloat16)
-        y = jnp.dot(cot_t, scaled, preferred_element_type=jnp.float32).T
+        return jnp.dot(cot_t, scaled, preferred_element_type=jnp.float32).T
+
+    def product_all(c):
+        y = product(c)
         for g in range(group):
             prod[c * group + g] = encode(y[g * size : (g + 1) * size])
 
+    def value(block):
+        return product(block) if group == 1 else decode(prod[block])
+
     def copy1(j, k):
         z = plane(j)
+        block = (diagonal, near_one(j), near_two(j))[k]
+        to = near_two(j) if k == 2 else near_one(j)
         return remote(
-            prod.at[z * q + peer(k)], got1.at[(k - 1) * m + z],
-            s1.at[(k - 1) * m + z], r1.at[(k - 1) * m + z], (mz * q + peer(k), ten),
+            prod.at[z * q + block], got1.at[k * m + z],
+            s1.at[k * m + z], r1.at[k * m + z], (mz * q + to, ten),
         )
 
     if group > 1:
-        loop(0, chunks, product)
+        loop(0, chunks, product_all)
 
     def stage1(j):
-        for k in range(1, q):
+        for k, block in enumerate((diagonal, near_one(j))):
             if group == 1:
-                product(plane(j) * q + peer(k))
+                prod[plane(j) * q + block] = encode(product(plane(j) * q + block))
             copy1(j, k).start()
 
-    loop(1, m + 1, stage1)
+    def stage1_sum(j):
+        z = plane(j)
+        block = z * q + near_two(j)
+        mine = value(block)
+        copy1(j, 0).wait_recv()
+        prod[block] = encode(mine + decode(got1[z]))
+        copy1(j, 2).start()
+
+    if q > 1:
+        loop(1, m + 1, stage1)
+        loop(1, m + 1, stage1_sum)
 
     local_copies[0].wait()
     total_row = jnp.zeros((rows, 128), jnp.float32)
@@ -179,19 +220,17 @@
 
     loop(1, n, lambda j: i_copy(j).start())
 
-    if group == 1:
-        loop(1, m + 1, lambda j: product(plane(j) * q + mp))
-
     def copy2(j):
         return remote(
             give2.at[j], got2.at[j], s2.at[j], r2.at[j], (plane(j) * q + mp, ten)
         )
 
     def plane_sum(j):
-        total = decode(prod[plane(j) * q + mp])
-        for k in range(1, q):
-            copy1(j, k).wait_recv()
-            total = total + decode(got1[(k - 1) * m + plane(j)])
+        total = value(plane(j) * q + mp)
+        if q > 1:
+            for k in (1, 2):
+                copy1(j, k).wait_recv()
+                total = total + decode(got1[k * m + plane(j)])
         return total
 
     def stage2(j):
@@ -209,7 +248,7 @@
     key_grad = plane_sum(m)
     for copy in local_copies[1:]:
         copy.wait()
-    kw_t = kw[...].astype(jnp.float32).T / gain_in[me]
+    kw_t = kw[...].astype(jnp.float32).T / gain_in[...]
 
     loop(1, n, lambda j: i_copy(j).wait_recv())
     mate_take.wait_recv()
@@ -257,56 +296,109 @@
     master_new, moment_new, second_new = adam_update(
         key_grad * clip, master[...], moment[...], second[...], 0.1
     )
-    master_out[...] = master_new
-    moment_out[...] = moment_new
-    second_out[...] = second_new
+    master_v[...] = master_new
+    moment_v[...] = moment_new
+    second_v[...] = second_new
     weight = master_new.astype(jnp.bfloat16)
     gain_new, gain_moment_new, gain_second_new = adam_update(
         gain_grad * clip[:, 0:1], gmaster[...], gmoment[...], gsecond[...], 0.0
     )
-    gmaster_out[...] = gain_new
-    gmoment_out[...] = gain_moment_new
-    gsecond_out[...] = gain_second_new
+    gmaster_v[...] = gain_new
+    gmoment_v[...] = gain_moment_new
+    gsecond_v[...] = gain_second_new
+    results = [
+        pltpu.make_async_copy(src, dst, out_sem.at[i])
+        for i, (src, dst) in enumerate([
+            (master_v, master_out), (moment_v, moment_out), (second_v, second_out),
+            (gmaster_v, gmaster_out), (gmoment_v, gmoment_out), (gsecond_v, gsecond_out),
+        ])
+    ]
+    for copy in results:
+        copy.start()
     gain = gain_new.astype(jnp.bfloat16).astype(jnp.float32)
 
     def keys(s):
         mixed = (resc[s] * gain).astype(jnp.bfloat16)
         return jnp.dot(mixed, weight, preferred_element_type=jnp.float32)
 
-    def p_copy(j):
-        return remote(part.at[j], got_part.at[j], sp.at[j], rp.at[j], (other(j), ten))
+    def a_copy(j, k):
+        at = (k - 1) * m + plane(j)
+        return remote(
+            part.at[at], got_part.at[at], sp.at[at], rp.at[at], (mz * q + peer(k), ten)
+        )
 
     def share(j):
-        part[j] = keys(other(j))
-        p_copy(j).start()
-
-    loop(1, n, share)
-    part[0] = keys(me)
-
-    def collect(j):
-        p_copy(j).wait_recv()
-        part[0] = part[0] + got_part[j]
-
-    loop(1, n, collect)
-    keys_out[...] = part[0].astype(jnp.bfloat16)
+        for k in range(1, q):
+            part[(k - 1) * m + plane(j)] = keys(plane(j) * q + peer(k))
+            a_copy(j, k).start()
+
+    loop(1, m + 1, share)
+
+    def b_copy(j):
+        dev = (plane(j) * q + mp, ten)
+        return remote(give_keys.at[j], got_keys.at[j], s3.at[j], r3.at[j], dev)
+
+    def plane_keys(j):
+        total = keys(plane(j) * q + mp)
+        for k in range(1, q):
+            a_copy(j, k).wait_recv()
+            total = total + got_part[(k - 1) * m + plane(j)]
+        return total
+
+    def pass_on(j):
+        give_keys[j] = plane_keys(j)
+        b_copy(j).start()
+
+    loop(1, m, pass_on)
+    keys_sum = plane_keys(m)
+    for j in range(1, m):
+        b_copy(j).wait_recv()
+        keys_sum = keys_sum + got_keys[j]
+    keys_v[...] = keys_sum.astype(jnp.bfloat16)
+    keys_copy = pltpu.make_async_copy(keys_v, keys_out, out_sem.at[6])
+    keys_copy.start()
 
     def drain(j):
         h_copy(j).wait_send()
         i_copy(j).wait_send()
         t_copy(j).wait_send()
-        p_copy(j).wait_send()
 
     loop(1, n, drain)
 
     def drain1(j):
         for k in range(1, q):
-            copy1(j, k).wait_send()
+            copy1(j, k - 1).wait_send()
+            a_copy(j, k).wait_send()
 
     loop(1, m + 1, drain1)
-    loop(1, m, lambda j: copy2(j).wait_send())
+    def drain2(j):
+        copy2(j).wait_send()
+        b_copy(j).wait_send()
+
+    loop(1, m, drain2)
     mate_give.wait_send()
     for t in range(1, heads):
         g_copy(t).wait_send()
+    for copy in results:
+        copy.wait()
+    keys_copy.wait()
+
+
+def hand_over(*refs):
+    count = 7
+    given, taken, held = refs[:count], refs[count : 2 * count], refs[2 * count : 3 * count]
+    sems = refs[-1]
+    loads = [pltpu.make_async_copy(given[i], held[i], sems.at[i]) for i in range(count)]
+    stores = [
+        pltpu.make_async_copy(held[i], taken[i], sems.at[count + i]) for i in range(count)
+    ]
+    for copy in loads:
+        copy.start()
+    for load, store in zip(loads, stores):
+        load.wait()
+        store.start()
+    for copy in stores:
+        copy.wait()
 
 
 def local(
@@ -341,18 +433,18 @@
         blocks = next_input.reshape(rows, n, size).transpose(1, 0, 2)
     gain = norm_gain.astype(jnp.float32)
     hbm = pl.BlockSpec(memory_space=pl.ANY)
-    vmem = pl.BlockSpec(memory_space=pltpu.VMEM)
     f32, bf16 = jnp.float32, jnp.bfloat16
     dma = pltpu.SemaphoreType.DMA
     shard = jax.ShapeDtypeStruct((size, cols), f32)
     line = jax.ShapeDtypeStruct((1, size), f32)
+    shapes = (
+        jax.ShapeDtypeStruct((rows, cols), bf16), shard, shard, shard, line, line, line,
+    )
     outs = pl.pallas_call(
         functools.partial(kernel, dims),
-        out_shape=(
-            jax.ShapeDtypeStruct((rows, cols), bf16), shard, shard, shard, line, line, line,
-        ),
-        in_specs=[hbm, hbm, hbm, vmem, vmem, hbm, hbm, hbm, vmem, vmem, vmem, hbm, hbm],
-        out_specs=(vmem,) * 7,
+        out_shape=shapes,
+        in_specs=[hbm] * 13,
+        out_specs=(hbm,) * 7,
         scratch_shapes=[
             pltpu.VMEM((chunks, tokens, width), bf16),
             pltpu.VMEM((tokens, cols), bf16),
@@ -370,9 +462,23 @@
             pltpu.VMEM((n, 8, 128), f32),
             pltpu.VMEM((heads, 8, size), f32),
             pltpu.VMEM((n, 8, 128), f32),
-            pltpu.VMEM((n, rows, cols), f32),
-            pltpu.VMEM((n, rows, cols), f32),
-            dma((chunks,)), dma((6,)), dma,
+            pltpu.VMEM((max(q - 1, 1) * m, rows, cols), f32),
+            pltpu.VMEM((max(q - 1, 1) * m, rows, cols), f32),
+            pltpu.VMEM((m, rows, cols), f32),
+            pltpu.VMEM((m, rows, cols), f32),
+            pltpu.VMEM((chunks, 1, width), f32),
+            pltpu.VMEM((1, size), f32),
+            pltpu.VMEM((1, size), f32),
+            pltpu.VMEM((1, size), f32),
+            pltpu.VMEM((1, size), f32),
+            pltpu.VMEM((rows, cols), bf16),
+            pltpu.VMEM((size, cols), f32),
+            pltpu.VMEM((size, cols), f32),
+            pltpu.VMEM((size, cols), f32),
+            pltpu.VMEM((1, size), f32),
+            pltpu.VMEM((1, size), f32),
+            pltpu.VMEM((1, size), f32),
+            dma((chunks,)), dma((11,)), dma,
             dma((max(q - 1, 1) * m,)), dma((max(q - 1, 1) * m,)),
             dma((m,)), dma((m,)),
             dma((n,)), dma((n,)),
@@ -380,10 +486,11 @@
             dma((n,)), dma((n,)),
             dma((heads,)), dma((heads,)),
             dma((n,)), dma((n,)),
-            dma((n,)), dma((n,)),
+            dma((max(q - 1, 1) * m,)), dma((max(q - 1, 1) * m,)),
+            dma((m,)), dma((m,)), dma((7,)),
         ],
         compiler_params=pltpu.CompilerParams(
-            collective_id=0, has_side_effects=True, vmem_limit_bytes=52 * 1024 * 1024
+            collective_id=0, has_side_effects=True, vmem_limit_bytes=64 * 1024 * 1024
         ),
         cost_estimate=pl.CostEstimate(
             flops=2 * tokens * depth * cols + 2 * n * rows * size * cols,
@@ -396,6 +503,14 @@
         gain_master.reshape(1, size), gain_moment.reshape(1, size),
         gain_second.reshape(1, size), next_input, blocks,
     )
+    outs = pl.pallas_call(
+        hand_over,
+        out_shape=shapes,
+        in_specs=[hbm] * 7,
+        out_specs=(hbm,) * 7,
+        scratch_shapes=[pltpu.VMEM(o.shape, o.dtype) for o in shapes] + [dma((14,))],
+        compiler_params=pltpu.CompilerParams(vmem_limit_bytes=64 * 1024 * 1024),
+    )(*outs)
     keys, master, moment, second, gmaster, gmoment, gsecond = outs
     return (
         keys, master, moment, second,

time: 72.5 us -> 63.5 us (0.88)
  the two profiles are of different devices: /device:TPU:14 before, /device:TPU:0 now
where the time goes in v2:
time: 63.5 us; the launch traced here: 63.1 us
  Pallas kernels  61.1 us (96%)
  other arithmetic  1.34 us (2%)
  between operations  0.64 us (1%)
    pallas_call x1, Pallas kernels, local(): pl.pallas_call(functools.partial(kernel, dims), out_shape=shapes, in_spec...  59.2 us
    pallas_call x1, Pallas kernels, local(): pl.pallas_call(hand_over, out_shape=shapes, in_specs=[hbm] * 7, out_specs...  1.97 us
    reshape x1, other arithmetic, local(): gain.reshape(chunks, 1, width)  1.34 us

profile of v2, /device:TPU:0, one launch (start us, length us, event | category | flops | bytes accessed | tf_op | source)
XLA Modules:
  0.0 63.1 jit_solution(7816674922622950101)
XLA Ops:
  0.6 1.3 %reshape.46 = f32[8192]{0:T(1024)} convert(bf16[8192]{0:T(1024)(128)(2,1)} %param.14) | non-fusion elementwise | flops 8192 | bytes 49152 | tf_op jit(solution)/shard_map/reshape | solution.py:502
  2.0 59.2 %shard_map.162 = (bf16[64,128]{1,0:T(8,128)(2,1)}, f32[512,128]{1,0:T(8,128)}, f32[512,128]{1,0:T(8,128)}, f32[512,128]{1,0:T(8,128)}, f32[1,512]{1,0:T(1,128)}, /*index=5*/f32[1,512]{1,0:T(1,128)}, f32[1,512]{1,0:T(1,128)}) custom-call(bf16[512,8192]{1,0:T(8,128)(2,1)} %normed.1, bf16[512,128]{1,0:T(8,128)(2,1)} %cot_in.1, bf16[8192,128]{1,0:T(8,128)(2,1)} %weight_in.1, ...), custom_call_target="tpu_custom_call" | custom-call | flops 1207959552 | bytes 8388608 | tf_op jit(solution)/shard_map/pallas_call | solution.py:443
  61.1 2.0 %shard_map.163 = (bf16[64,128]{1,0:T(8,128)(2,1)}, f32[512,128]{1,0:T(8,128)}, f32[512,128]{1,0:T(8,128)}, f32[512,128]{1,0:T(8,128)}, f32[1,512]{1,0:T(1,128)}, /*index=5*/f32[1,512]{1,0:T(1,128)}, f32[1,512]{1,0:T(1,128)}) custom-call(bf16[64,128]{1,0:T(8,128)(2,1)} %get-tuple-element.21.refs_0_, f32[512,128]{1,0:T(8,128)} %get-tuple-element.22.refs_1_, ...), custom_call_target="tpu_custom_call" | custom-call | tf_op jit(solution)/shard_map/pallas_call | solution.py:506

commit v3 on v2

--- a/solution.py
+++ b/solution.py
@@ -44,7 +44,7 @@
     xbuf, cot, kw, master, moment, second, rows_in, prod, got1, give2, got2,
     hbuf, resc, inv_all, gain_all, total_all, part, got_part, give_keys, got_keys,
     gains, gain_in, gmaster, gmoment, gsecond, keys_v, master_v, moment_v, second_v,
-    gmaster_v, gmoment_v, gsecond_v,
+    gmaster_v, gmoment_v, gsecond_v, gains_raw,
     x_sem, in_sem, own_sem, s1, r1, s2, r2, sh, rh, sm, rm, si, ri, sg, rg, st, rt, sp, rp, s3, r3, out_sem,
 ):
     n, heads, q, m, size, width, group, chunks, rows, half_rows = dims
@@ -86,7 +86,9 @@
 
     cot_copy = pltpu.make_async_copy(cot_in, cot, in_sem.at[0])
     cot_copy.start()
-    gains_copy = pltpu.make_async_copy(gains_in, gains, in_sem.at[6])
+    gains_copy = pltpu.make_async_copy(
+        gains_in, gains_raw if group == 1 else gains, in_sem.at[6]
+    )
     gains_copy.start()
     if group == 1:
 
@@ -107,11 +109,14 @@
         pltpu.make_async_copy(master_in, master, in_sem.at[3]),
         pltpu.make_async_copy(moment_in, moment, in_sem.at[4]),
         pltpu.make_async_copy(second_in, second, in_sem.at[5]),
-        pltpu.make_async_copy(gain_in_hbm.at[me], gain_in, in_sem.at[7]),
         pltpu.make_async_copy(gmaster_in, gmaster, in_sem.at[8]),
         pltpu.make_async_copy(gmoment_in, gmoment, in_sem.at[9]),
         pltpu.make_async_copy(gsecond_in, gsecond, in_sem.at[10]),
     ]
+    if group > 1:
+        local_copies.append(
+            pltpu.make_async_copy(gain_in_hbm.at[me], gain_in, in_sem.at[7])
+        )
     for copy in local_copies:
         copy.start()
 
@@ -152,10 +157,16 @@
             next_block(other(j)), hbuf.at[half, me], sh.at[j], rh.at[j], (other(j), ten)
         )
 
-    loop(1, n, lambda j: h_copy(j).start())
+    def h_plane(j):
+        for k in range(1 if j is m else 0, q):
+            h_copy(lax.rem(plane(j) * q + peer(k) - me + n, n)).start()
+
 
     cot_copy.wait()
     gains_copy.wait()
+    if group == 1:
+        for c in range(chunks):
+            gains[c, 0] = gains_raw[c * width : (c + 1) * width].astype(jnp.float32)
     cot_t = cot[...].astype(jnp.float32).T.astype(jnp.bfloat16)
 
     def product(c):
@@ -197,8 +208,14 @@
         prod[block] = encode(mine + decode(got1[z]))
         copy1(j, 2).start()
 
+    def stage1_send(j):
+        if q > 1:
+            stage1(j)
+        h_plane(j)
+
+    loop(1, m, stage1_send)
+    stage1_send(m)
     if q > 1:
-        loop(1, m + 1, stage1)
         loop(1, m + 1, stage1_sum)
 
     local_copies[0].wait()
@@ -248,7 +265,7 @@
     key_grad = plane_sum(m)
     for copy in local_copies[1:]:
         copy.wait()
-    kw_t = kw[...].astype(jnp.float32).T / gain_in[...]
+    kw_t = kw[...].astype(jnp.float32).T / (gains[me] if group == 1 else gain_in[...])
 
     loop(1, n, lambda j: i_copy(j).wait_recv())
     mate_take.wait_recv()
@@ -317,19 +334,20 @@
         copy.start()
     gain = gain_new.astype(jnp.bfloat16).astype(jnp.float32)
 
-    def keys(s):
-        mixed = (resc[s] * gain).astype(jnp.bfloat16)
-        return jnp.dot(mixed, weight, preferred_element_type=jnp.float32)
+    def keys(z):
+        mixed = (resc[pl.ds(z * q, q)] * gain).astype(jnp.bfloat16).reshape(q * rows, size)
+        made = jnp.dot(mixed, weight, preferred_element_type=jnp.float32)
+        part[pl.ds(z * q, q)] = made.reshape(q, rows, -1)
 
     def a_copy(j, k):
         at = (k - 1) * m + plane(j)
         return remote(
-            part.at[at], got_part.at[at], sp.at[at], rp.at[at], (mz * q + peer(k), ten)
+            part.at[plane(j) * q + peer(k)], got_part.at[at], sp.at[at], rp.at[at], (mz * q + peer(k), ten)
         )
 
     def share(j):
+        keys(plane(j))
         for k in range(1, q):
-            part[(k - 1) * m + plane(j)] = keys(plane(j) * q + peer(k))
             a_copy(j, k).start()
 
     loop(1, m + 1, share)
@@ -339,7 +357,7 @@
         return remote(give_keys.at[j], got_keys.at[j], s3.at[j], r3.at[j], dev)
 
     def plane_keys(j):
-        total = keys(plane(j) * q + mp)
+        total = part[plane(j) * q + mp]
         for k in range(1, q):
             a_copy(j, k).wait_recv()
             total = total + got_part[(k - 1) * m + plane(j)]
@@ -431,7 +449,11 @@
         blocks = next_input
     else:
         blocks = next_input.reshape(rows, n, size).transpose(1, 0, 2)
-    gain = norm_gain.astype(jnp.float32)
+    if group == 1:
+        gains = own_gains = norm_gain
+    else:
+        gain = norm_gain.astype(jnp.float32)
+        gains, own_gains = gain.reshape(chunks, 1, width), gain.reshape(n, 1, size)
     hbm = pl.BlockSpec(memory_space=pl.ANY)
     f32, bf16 = jnp.float32, jnp.bfloat16
     dma = pltpu.SemaphoreType.DMA
@@ -462,7 +484,7 @@
             pltpu.VMEM((n, 8, 128), f32),
             pltpu.VMEM((heads, 8, size), f32),
             pltpu.VMEM((n, 8, 128), f32),
-            pltpu.VMEM((max(q - 1, 1) * m, rows, cols), f32),
+            pltpu.VMEM((n, rows, cols), f32),
             pltpu.VMEM((max(q - 1, 1) * m, rows, cols), f32),
             pltpu.VMEM((m, rows, cols), f32),
             pltpu.VMEM((m, rows, cols), f32),
@@ -478,6 +500,7 @@
             pltpu.VMEM((1, size), f32),
             pltpu.VMEM((1, size), f32),
             pltpu.VMEM((1, size), f32),
+            pltpu.VMEM((depth,), bf16),
             dma((chunks,)), dma((11,)), dma,
             dma((max(q - 1, 1) * m,)), dma((max(q - 1, 1) * m,)),
             dma((m,)), dma((m,)),
@@ -499,7 +522,7 @@
         ),
     )(
         normed, key_cot, key_weight,
-        gain.reshape(chunks, 1, width), gain.reshape(n, 1, size), weight_master, weight_moment, weight_second,
+        gains, own_gains, weight_master, weight_moment, weight_second,
         gain_master.reshape(1, size), gain_moment.reshape(1, size),
         gain_second.reshape(1, size), next_input, blocks,
     )

time: 63.5 us -> 62.5 us (0.984)
  other arithmetic: 1.34 us -> 0 us
    reshape x1 -> x0, other arithmetic: 1.34 us -> none  [local(): gain.reshape(chunks, 1, width)]
where the time goes in v3:
time: 62.5 us; the launch traced here: 62.2 us
  Pallas kernels  61.6 us (99%)
  between operations  0.64 us (1%)
    pallas_call x1, Pallas kernels, local(): pl.pallas_call(functools.partial(kernel, dims), out_shape=shapes, in_spec...  59.6 us
    pallas_call x1, Pallas kernels, local(): pl.pallas_call(hand_over, out_shape=shapes, in_specs=[hbm] * 7, out_specs...  1.97 us

profile of v3, /device:TPU:0, one launch (start us, length us, event | category | flops | bytes accessed | tf_op | source)
XLA Modules:
  0.0 62.2 jit_solution(13595100080439279470)
XLA Ops:
  0.6 59.6 %shard_map.162 = (bf16[64,128]{1,0:T(8,128)(2,1)}, f32[512,128]{1,0:T(8,128)}, f32[512,128]{1,0:T(8,128)}, f32[512,128]{1,0:T(8,128)}, f32[1,512]{1,0:T(1,128)}, /*index=5*/f32[1,512]{1,0:T(1,128)}, f32[1,512]{1,0:T(1,128)}) custom-call(bf16[512,8192]{1,0:T(8,128)(2,1)} %normed.1, bf16[512,128]{1,0:T(8,128)(2,1)} %cot_in.1, bf16[8192,128]{1,0:T(8,128)(2,1)} %weight_in.1, ...), custom_call_target="tpu_custom_call" | custom-call | flops 1207959552 | bytes 8388608 | tf_op jit(solution)/shard_map/pallas_call | solution.py:465
  60.3 2.0 %shard_map.163 = (bf16[64,128]{1,0:T(8,128)(2,1)}, f32[512,128]{1,0:T(8,128)}, f32[512,128]{1,0:T(8,128)}, f32[512,128]{1,0:T(8,128)}, f32[1,512]{1,0:T(1,128)}, /*index=5*/f32[1,512]{1,0:T(1,128)}, f32[1,512]{1,0:T(1,128)}) custom-call(bf16[64,128]{1,0:T(8,128)(2,1)} %get-tuple-element.21.refs_0_, f32[512,128]{1,0:T(8,128)} %get-tuple-element.22.refs_1_, ...), custom_call_target="tpu_custom_call" | custom-call | tf_op jit(solution)/shard_map/pallas_call | solution.py:529
